TPU v7x, 768 devices: a whole 4x8x12 slice. The times are simulated.
768 devices in a mesh: dom: 48 (over z, x), feat: 16 (over y, core).
Axes of the slice: x: 4, y: 8, z: 12, core: 2. Of those that a mesh axis runs over, the one named last changes fastest.
Arguments:
- features: float32 [256, 98304], P('feat', 'dom'), may hold values from -6 to 6
- tile_vals: float32 [768, 6, 128, 128], P(('dom', 'feat')), may hold values from -0.21875 to 0.21875
- tile_src: int32 [768, 6], P(('dom', 'feat')), may hold values from 0 to 33, as said below
- tile_count: int32 [768], P(('dom', 'feat')), may hold values from 3 to 6, as said below
- send_rows: int32 [2304, 32], P('dom'), may hold values from 0 to 2047
- hub_owner: int32 [768], replicated, may hold values from 0 to 47, as said below
- hub_row: int32 [768], replicated, may hold values from 0 to 2047
- weight: float32 [256, 256], P(None, 'feat'), may hold values from -0.375 to 0.375
- cotangent: float32 [256, 98304], P(None, ('dom', 'feat')), may hold values from -0.01953125 to 0.01953125
Outputs:
- output: float32 [256, 98304], P(None, ('dom', 'feat'))
- grad_weight: float32 [256, 256], P(None, 'feat')
Inputs may be any that keep to these rules, and one draw needn't show every extreme that they name: `tile_src`: slot 0 of destination tile t of a partition names that partition's own tile t, slot 1 a boundary tile (indices 16 up to the first hub tile), slot 2 a hub tile (the last ones); other slots any source tile. `tile_count`: some partition has all its destination tiles at 6 live slots. `hub_owner`: each partition owns at most 48 hub vertices, and some partition owns exactly 48.
All inputs are finite; a program needn't handle non-finite values.
Results may differ from a plain program's by a relative error of at most 0.0003.
Values sent between devices are 32-bit elements; how exact they have to be, the bound alone decides.
A program may use at most 32 MiB of HBM per device.

v0:
```python
import jax
import jax.numpy as jnp
from jax import lax
from jax.sharding import PartitionSpec as P


def on_device(
    features, tile_vals, tile_src, tile_count, send_rows, hub_owner, hub_row, weight, cotangent
):
    feat_share, node_dev = features.shape
    slot_count = tile_vals.shape[1]
    tile_len = tile_vals.shape[2]
    my_index = lax.axis_index("dom")
    outgoing = features[:, send_rows]
    arrived = lax.all_to_all(outgoing, "dom", split_axis=1, concat_axis=1, tiled=True)
    owned_here = hub_owner == my_index
    picked_hubs = jnp.where(owned_here[None, :], features[:, hub_row], 0.0)
    hub_block = lax.psum(picked_hubs, "dom")
    source = jnp.concatenate([features, arrived.reshape(feat_share, -1), hub_block], axis=1)
    source_full = lax.all_gather(source, "feat", axis=0, tiled=True)
    feat_width = source_full.shape[0]
    source_full = source_full.reshape(feat_width, -1, tile_len)
    gathered_tiles = source_full[:, tile_src]
    live_mask = (jnp.arange(slot_count, dtype=jnp.int32)[None, :] < tile_count[:, None]).astype(
        jnp.float32
    )
    gathered_tiles = gathered_tiles * live_mask[None, :, :, None]
    aggregated = jnp.einsum(
        "ftkj,tkji->fti", gathered_tiles, tile_vals, precision=lax.Precision.HIGHEST
    ).reshape(feat_width, -1)
    full_weight = lax.all_gather(weight, "feat", axis=1, tiled=True)
    output = jnp.tanh(
        lax.dot_general(
            full_weight, aggregated, (((0,), (0,)), ((), ())), precision=lax.Precision.HIGHEST
        )
    )
    pre_grad = cotangent * (1.0 - output * output)
    partial_grad = lax.dot_general(
        aggregated, pre_grad, (((1,), (1,)), ((), ())), precision=lax.Precision.HIGHEST
    )
    column_share = weight.shape[1]
    grad_whole = lax.psum(partial_grad, ("dom", "feat"))
    grad_weight = lax.dynamic_slice_in_dim(
        grad_whole, lax.axis_index("feat") * column_share, column_share, 1
    )
    return (output, grad_weight)


def solution(mesh):
    in_specs = (
        P("feat", "dom"),
        P(("dom", "feat"), None, None, None),
        P(("dom", "feat"), None),
        P(("dom", "feat")),
        P("dom", None),
        P(),
        P(),
        P(None, "feat"),
        P(None, ("dom", "feat")),
    )
    out_specs = (P(None, ("dom", "feat")), P(None, "feat"))
    return jax.shard_map(
        on_device, mesh=mesh, in_specs=in_specs, out_specs=out_specs, check_vma=False
    )
```

profile of v0, /device:TPU:1, one launch (start us, length us, event | category | flops | bytes accessed | tf_op | source)
XLA Modules:
  0.0 781.6 jit_solution(7678803490334833188)
XLA Ops:
  7.2 1.3 copy.27
  8.5 0.7 compare_select_fusion
  9.2 0.1 copy.26
  9.3 0.1 reshape.38
  9.4 2.6 gather_fusion
  12.0 0.3 copy.28
  12.3 0.8 reshape.66
  13.2 18.8 %all-to-all-start = ((f32[48,1,512]{2,1,0:T(1,128)}), f32[48,1,512]{2,1,0:T(1,128)S(1)}, u32[]{:S(2)}, u32[]{:S(2)}) async-start(f32[48,1,512]{2,1,0:T(1,128)} %reshape.66), calls=%async_computation | async-start | bytes 196608 | tf_op jit(solution)/shard_map/all_to_all | solution.py:15
  32.0 0.0 all-gather.2.cloned.1.call-start
  32.1 1.6 gather_fusion.1
  33.7 0.2 select_bitcast_fusion
  33.9 171.5 %psum.14 = f32[16,768]{0,1:T(8,128)S(1)} all-reduce(f32[16,768]{0,1:T(8,128)S(1)} %select_bitcast_fusion), channel_id=1, replica_groups=mesh['dom'=48,'feat'=16] {'dom'}, use_global_device_ids=true, to_apply=%region_0.1 | all-reduce | flops 12288 | bytes 98304 | tf_op jit(solution)/shard_map/psum | solution.py:18
  205.4 0.1 copy.31
  205.5 0.5 broadcast.44
  206.1 0.9 reduce
  207.0 0.1 reshape.67
  207.1 0.1 copy.29
  207.2 0.2 reshape.33
  207.4 0.7 pad_maximum_fusion
  208.2 0.0 all-reduce.2.cloned.1.call-start
  208.9 0.1 copy.34
  209.1 60.9 %all_gather.7 = f32[256,256]{0,1:T(8,128)S(1)} all-gather(f32[256,16]{0,1:T(8,128)S(1)} %copy-done.3), channel_id=1, replica_groups=mesh['dom'=48,'feat'=16] {'feat'}, dimensions={1}, use_global_device_ids=true | all-gather | bytes 278528 | tf_op jit(solution)/shard_map/all_gather | solution.py:31
  270.0 25.4 %all-gather.2.cloned.1.call-done = f32[256,4352]{1,0:T(8,128)} async-done(((f32[16,4352]{1,0:T(8,128)}), f32[256,4352]{1,0:T(8,128)}) %all-gather.2.cloned.1.call-update) | async-done | bytes 4456464 | tf_op jit(solution)/shard_map/all_gather | solution.py:20
  295.4 5.8 copy.32
  301.2 5.7 copy.33
  306.8 2.9 gather_fusion.2
  309.7 0.8 convolution_bitcast_fusion
  310.6 0.4 fusion
  311.0 1.1 fusion.5
  312.1 0.8 copy.35
  312.9 460.6 %all-reduce.2.cloned.1.call-done = f32[256,256]{0,1:T(8,128)} async-done(((f32[256,256]{0,1:T(8,128)}), f32[256,256]{0,1:T(8,128)}) %all-reduce.2.cloned.1.call-update) | async-done | bytes 262160 | tf_op jit(solution)/shard_map/psum | solution.py:42
  773.5 1.3 constant_dynamic-slice_fusion
  (25 shorter events, 0.1 us)
Async XLA Ops:
  7.2 302.6 %copy-start = (f32[1,6,128,128]{3,2,1,0:T(8,128)S(1)}, f32[1,6,128,128]{3,2,1,0:T(8,128)}, u32[]{:S(2)}) copy-start(f32[1,6,128,128]{3,2,1,0:T(8,128)} %param.10) | copy-start | bytes 1179652
  7.2 24.9 %copy-start.4 = (s32[768]{0:T(1024)S(1)}, s32[768]{0:T(1024)}, u32[]{:S(2)}) copy-start(s32[768]{0:T(1024)} %param.15) | copy-start | bytes 9220
  7.2 24.9 %copy-start.5 = (s32[768]{0:T(1024)S(1)}, s32[768]{0:T(1024)}, u32[]{:S(2)}) copy-start(s32[768]{0:T(1024)} %param.14) | copy-start | bytes 9220
  9.4 198.0 %copy-start.1 = (f32[16,2048]{1,0:T(8,128)S(1)}, f32[16,2048]{1,0:T(8,128)}, u32[]{:S(2)}) copy-start(f32[16,2048]{1,0:T(8,128)} %param.9) | copy-start | bytes 393220
  12.0 196.9 %copy-start.2 = (f32[256,128]{1,0:T(8,128)S(1)}, f32[256,128]{1,0:T(8,128)}, u32[]{:S(2)}) copy-start(f32[256,128]{1,0:T(8,128)} %param.17) | copy-start | bytes 393220
  12.0 197.0 %copy-start.6 = (s32[1,6]{1,0:T(1,128)S(1)}, s32[1,6]{1,0:T(1,128)}, u32[]{:S(2)}) copy-start(s32[1,6]{1,0:T(1,128)} %param.11) | copy-start | bytes 76
  12.0 197.0 %copy-start.3 = (f32[256,16]{0,1:T(8,128)S(1)}, f32[256,16]{0,1:T(8,128)}, u32[]{:S(2)}) copy-start(f32[256,16]{0,1:T(8,128)} %param.16) | copy-start | bytes 49156
  13.2 192.4 %all-to-all-start = ((f32[48,1,512]{2,1,0:T(1,128)}), f32[48,1,512]{2,1,0:T(1,128)S(1)}, u32[]{:S(2)}, u32[]{:S(2)}) async-start(f32[48,1,512]{2,1,0:T(1,128)} %reshape.66), calls=%async_computation | async-start | bytes 196608 | tf_op jit(solution)/shard_map/all_to_all | solution.py:15
  32.0 263.3 %all-gather.2.cloned.1.call-start = ((), (), s32[]{:S(2)}) async-start(), calls=%async_computation.1 | async-start | bytes 4734976 | tf_op jit(solution)/shard_map/all_gather | solution.py:20
  208.2 565.3 %all-reduce.2.cloned.1.call-start = ((), (), s32[]{:S(2)}) async-start(), calls=%async_computation.2 | async-start | bytes 524288 | tf_op jit(solution)/shard_map/psum | solution.py:42
Sparse Core Ops, SparseCore 0:
  208.3 86.9 all-gather.1
  312.2 461.1 all-reduce.1
where the time goes:
time: 782 us
  waiting for transfers between devices  486 us (62%)
  blocking collectives  232 us (30%)
  local copies, waits for them, and re-layouts  24.4 us (3%)
  starting transfers between devices  18.9 us (2%)
  between operations  15 us (2%)
    psum x1, waiting for transfers between devices, on_device(): grad_whole = lax.psum(partial_grad, ('dom', 'feat'))  461 us
    psum x1, blocking collectives, on_device(): hub_block = lax.psum(picked_hubs, 'dom')  172 us
    all_gather x1, blocking collectives, on_device(): full_weight = lax.all_gather(weight, 'feat', axis=1, tiled=True)  60.9 us
    all_gather x1, waiting for transfers between devices, on_device(): source_full = lax.all_gather(source, 'feat', axis=0, tiled=True)  25.4 us
    all_to_all x1, starting transfers between devices, on_device(): lax.all_to_all(outgoing, 'dom', split_axis=1, concat_axis=1, tiled=True)  18.8 us
  transfers between devices with their start and end apart: 3, of which 2 were waited for; matrix products, arithmetic and copies ran while one was open for 0% of the time, Pallas kernels for 0%

commit v1 on v0

v1 whole, which is shorter than its diff:
```python
import jax
import jax.numpy as jnp
from jax import lax
from jax.experimental import pallas as pl
from jax.experimental.pallas import tpu as pltpu
from jax.sharding import PartitionSpec as P

N_X, N_Z, N_Y = 4, 12, 8
N_DOM = N_X * N_Z
N_FEAT = 2 * N_Y
D = 256
TILE = 128
SHARE = D // N_FEAT
SLOTS = 6
OWN = 16
BORDER = 12
HUB_TILES = 6
HUBS = HUB_TILES * TILE
EXT = OWN + BORDER + HUB_TILES
LIVE_FIRST = 3
F32, BF16, I32 = jnp.float32, jnp.bfloat16, jnp.int32


def split(value):
    high = value.astype(BF16)
    return high, (value - high.astype(F32)).astype(BF16)


def dot3(a, b, dims):
    a_high, a_low = split(a)
    b_high, b_low = split(b)

    def one(u, v):
        return lax.dot_general(u, v, (dims, ((), ())), preferred_element_type=F32)

    return one(a_high, b_high) + (one(a_high, b_low) + one(a_low, b_high))


def pick(table, index):
    return jnp.take_along_axis(table, index, axis=1, mode="promise_in_bounds")


def loop(first, last, body):
    def step(i, carry):
        body(i)
        return carry

    lax.fori_loop(first, last, step, 0)


def kernel(
    features, tile_src, tile_count, send_rows, hub_owner, hub_row, weight, tile_vals, cotangent,
    output, grad_weight,
    vals, cot, source, stage, picked, ints, ints_smem,
    border_out, border_in, hub_out, hub_z, hub_x, weight_t,
    core_out, core_in, y_out, y_in, x_out, x_in, z_out, z_in, last_in,
    local_sems, send_sems, recv_sems,
):
    dom, feat = lax.axis_index("dom"), lax.axis_index("feat")
    z, x = dom // N_X, dom % N_X
    y, core = feat // 2, feat % 2

    def dom_peer(j):
        return lax.rem(dom + j, N_DOM)

    def feat_peer(j):
        return lax.rem(feat + j, N_FEAT)

    def remote(src, dst, which, device):
        return pltpu.make_async_remote_copy(
            src_ref=src, dst_ref=dst, send_sem=send_sems.at[which], recv_sem=recv_sems.at[which],
            device_id=device, device_id_type=pl.DeviceIdType.MESH,
        )

    def wait_all(ref, sem):
        pltpu.make_async_copy(ref, ref, sem).wait()

    barrier = pltpu.get_barrier_semaphore()
    loop(1, N_DOM, lambda j: pl.semaphore_signal(
        barrier, inc=1, device_id={"dom": dom_peer(j)}, device_id_type=pl.DeviceIdType.MESH))
    loop(1, N_FEAT, lambda j: pl.semaphore_signal(
        barrier, inc=1, device_id={"feat": feat_peer(j)}, device_id_type=pl.DeviceIdType.MESH))

    vals_copy = pltpu.make_async_copy(tile_vals, vals, local_sems.at[0])
    cot_copy = pltpu.make_async_copy(cotangent, cot, local_sems.at[1])
    vals_copy.start()
    cot_copy.start()

    lane8 = lax.broadcasted_iota(I32, (8, TILE), 1)
    row8 = lax.broadcasted_iota(I32, (8, TILE), 0)

    for t in range(OWN):
        source[t] = features[:, t * TILE : (t + 1) * TILE]
    lane1 = lax.broadcasted_iota(I32, (1, TILE), 1)
    listed = jnp.zeros((1, TILE), I32)
    for k in range(SLOTS):
        listed = jnp.where(lane1 == k, tile_src[0, k], listed)
    ints[pl.ds(feat, 1)] = listed[None]
    weight_t[pl.ds(feat, 1)] = jnp.transpose(weight[...])[None]

    owner = hub_owner[...]
    earlier = (lax.broadcasted_iota(I32, (HUBS, HUBS), 0) < lax.broadcasted_iota(I32, (HUBS, HUBS), 1))
    owned = (lax.broadcasted_iota(I32, (N_DOM, HUBS), 0) == owner).astype(F32)
    before = jnp.dot(owned.astype(BF16), earlier.astype(F32).astype(BF16), preferred_element_type=F32)
    rank = jnp.dot(jnp.ones((8, N_DOM), BF16), (owned * before).astype(BF16), preferred_element_type=F32)
    rank = rank.astype(I32)
    mine = owner == dom
    place = lax.broadcasted_iota(I32, (TILE, HUBS), 0) % 64
    chosen = (mine & (rank[0:1] == place)).astype(F32).astype(BF16)
    row = hub_row[...]
    row_parts = jnp.concatenate([jnp.broadcast_to(row // 16, (8, HUBS)), jnp.broadcast_to(row % 16, (8, HUBS))], axis=0)
    my_rows = lax.dot_general(
        row_parts.astype(F32).astype(BF16), chosen, (((1,), (1,)), ((), ())), preferred_element_type=F32
    )
    my_rows = my_rows[0:8].astype(I32) * 16 + my_rows[8:16].astype(I32)

    def columns(v, index):
        low, high = index % TILE, index // TILE
        found = jnp.zeros((8, TILE), F32)
        for t in range(OWN):
            part = pick(features[8 * v : 8 * v + 8, t * TILE : (t + 1) * TILE], low)
            found = jnp.where(high == t, part, found)
        return found

    hub_out[...] = jnp.where(lane8 < 64, columns(0, my_rows), columns(1, my_rows))

    group4 = lax.broadcasted_iota(I32, (4, TILE), 1) // 32
    in_group = [group4 == (t + x) % 4 for t in range(4)]

    def border_tile(q):
        rows = jnp.broadcast_to(send_rows[pl.ds(q, 1), :], (8, TILE))
        quarter = []
        for v in range(2):
            turned = pick(rows, (lane8 - 32 * (2 * v + row8 // 4 + x)) % TILE)
            found = columns(v, turned)
            quarter += [found[0:4], found[4:8]]
        for d in range(4):
            message = quarter[0]
            for a in range(4):
                message = jnp.where(in_group[(a + d) % 4], quarter[a], message)
            border_out[pl.ds(4 * q + d, 1)] = message[None]

    loop(0, BORDER, border_tile)

    pl.semaphore_wait(barrier, N_DOM - 1 + N_FEAT - 1)

    def z_device(z_to):
        return {"dom": z_to * N_X + x}

    def x_device(x_to):
        return {"dom": z * N_X + x_to}

    def y_device(y_to):
        return {"feat": y_to * 2 + core}

    loop(1, N_Z, lambda j: remote(hub_out, hub_z.at[z], 0, z_device(lax.rem(z + j, N_Z))).start())
    loop(1, N_DOM, lambda j: remote(
        border_out.at[dom_peer(j)], border_in.at[dom], 1, {"dom": dom_peer(j)}).start())
    loop(1, N_FEAT, lambda j: remote(ints.at[feat], ints.at[feat], 2, {"feat": feat_peer(j)}).start())
    loop(1, N_FEAT, lambda j: remote(
        source.at[feat_peer(j)], picked.at[0, feat], 3, {"feat": feat_peer(j)}).start())
    loop(1, N_FEAT, lambda j: remote(weight_t.at[feat], weight_t.at[feat], 4, {"feat": feat_peer(j)}).start())

    picked[0, pl.ds(feat, 1)] = source[pl.ds(feat, 1)]
    border_in[pl.ds(dom, 1)] = border_out[pl.ds(dom, 1)]
    hub_z[pl.ds(z, 1)] = hub_out[...][None]

    wait_all(hub_z.at[pl.ds(0, N_Z - 1)], recv_sems.at[0])
    loop(1, N_X, lambda j: remote(hub_z, hub_x.at[x], 5, x_device(lax.rem(x + j, N_X))).start())
    hub_x[pl.ds(x, 1)] = hub_z[...][None]

    wait_all(ints.at[pl.ds(0, N_FEAT - 1)], recv_sems.at[2])
    ints_copy = pltpu.make_async_copy(ints, ints_smem, local_sems.at[2])
    ints_copy.start()

    wait_all(border_in.at[pl.ds(0, N_DOM - 1)], recv_sems.at[1])
    quarter_of = [2 * v + row8 // 4 for v in range(2)]

    def border_arrived(q):
        pieces = []
        for e in range(4):
            piece = border_in[pl.ds(4 * q + e, 1)][0]
            pieces.append(jnp.concatenate([piece, piece], axis=0))
        for v in range(2):
            mixed = pieces[0]
            for e in range(1, 4):
                mixed = jnp.where(lane8 // 32 == (quarter_of[v] + e + x) % 4, pieces[e], mixed)
            source[pl.ds(OWN + q, 1), 8 * v : 8 * v + 8] = pick(mixed, (lane8 + 32 * (quarter_of[v] + x)) % TILE)[None]

    loop(0, BORDER, border_arrived)

    wait_all(hub_x.at[pl.ds(0, N_X - 1)], recv_sems.at[5])
    owner8 = jnp.broadcast_to(owner, (8, HUBS))
    at = (owner8 % 2) * 64 + rank
    pair = owner8 // 2

    def hub_pair(p, found):
        even = hub_x[2 * (p % 2), p // 2]
        odd = hub_x[2 * (p % 2) + 1, p // 2]
        tables = (
            jnp.where(lane8 < 64, even, pltpu.roll(odd, 64, 1)),
            jnp.where(lane8 < 64, pltpu.roll(even, 64, 1), odd),
        )
        result = []
        for q in range(HUB_TILES):
            cut = slice(q * TILE, (q + 1) * TILE)
            for v in range(2):
                result.append(jnp.where(pair[:, cut] == p, pick(tables[v], at[:, cut]), found[2 * q + v]))
        return tuple(result)

    found = lax.fori_loop(0, N_DOM // 2, hub_pair, (jnp.zeros((8, TILE), F32),) * (2 * HUB_TILES))
    for q in range(HUB_TILES):
        for v in range(2):
            source[OWN + BORDER + q, 8 * v : 8 * v + 8] = found[2 * q + v]

    ints_copy.wait()

    def send_slots(first, last, which):
        def to_peer(j):
            peer = feat_peer(j)
            for k in range(first, last):
                stage[peer, k] = source[ints_smem[peer, 0, k]]
            cut = pl.ds(first, last - first)
            remote(stage.at[peer, cut], picked.at[cut, feat], which, {"feat": peer}).start()

        loop(1, N_FEAT, to_peer)
        for k in range(first, last):
            picked[k, feat] = source[tile_src[0, k]]

    send_slots(1, LIVE_FIRST, 6)
    send_slots(LIVE_FIRST, SLOTS, 7)

    vals_copy.wait()
    count = tile_count[0]

    def aggregate(k):
        live = jnp.where(k < count, 1.0, 0.0).astype(F32)
        return dot3(picked[k].reshape(D, TILE), vals[0, k] * live, ((1,), (0,)))

    def arrived(first, last, which):
        wait_all(picked.at[pl.ds(first, last - first), pl.ds(0, N_FEAT - 1)], recv_sems.at[which])

    arrived(0, 1, 3)
    aggregated = aggregate(0)
    arrived(1, LIVE_FIRST, 6)
    for k in range(1, LIVE_FIRST):
        aggregated += aggregate(k)
    wait_all(weight_t.at[pl.ds(0, N_FEAT - 1)], recv_sems.at[4])
    cot_copy.wait()
    arrived(LIVE_FIRST, SLOTS, 7)
    for k in range(LIVE_FIRST, SLOTS):
        aggregated += aggregate(k)

    result = jnp.tanh(dot3(weight_t[...].reshape(D, D), aggregated, ((1,), (0,))))
    output[...] = result
    pre_grad = cot[...] * (1.0 - result * result)
    partial = dot3(pre_grad, aggregated, ((1,), (1,)))

    for c in range(2):
        for w in range(N_Y):
            first = SHARE * (2 * w + c)
            core_out[c, w] = partial[first : first + SHARE]
    other = 1 - core
    to_core = remote(core_out.at[other], core_in, 8, {"feat": y * 2 + other})
    to_core.start()
    to_core.wait_recv()
    y_out[...] = core_out[core] + core_in[...]
    loop(1, N_Y, lambda j: remote(
        y_out.at[lax.rem(y + j, N_Y)], y_in.at[y], 9, y_device(lax.rem(y + j, N_Y))).start())
    y_in[pl.ds(y, 1)] = y_out[pl.ds(y, 1)]
    wait_all(y_in.at[pl.ds(0, N_Y - 1)], recv_sems.at[9])
    total = y_in[0]
    for w in range(1, N_Y):
        total += y_in[w]
    for j in range(N_X):
        x_out[j] = total[8 * (j // 2) : 8 * (j // 2) + 8, TILE * (j % 2) : TILE * (j % 2) + TILE]
    loop(1, N_X, lambda j: remote(
        x_out.at[lax.rem(x + j, N_X)], x_in.at[x], 10, x_device(lax.rem(x + j, N_X))).start())
    x_in[pl.ds(x, 1)] = x_out[pl.ds(x, 1)]
    wait_all(x_in.at[pl.ds(0, N_X - 1)], recv_sems.at[10])
    z_out[...] = (x_in[0] + x_in[1]) + (x_in[2] + x_in[3])
    loop(1, N_Z, lambda j: remote(z_out, z_in.at[z], 11, z_device(lax.rem(z + j, N_Z))).start())
    z_in[pl.ds(z, 1)] = z_out[...][None]
    wait_all(z_in.at[pl.ds(0, N_Z - 1)], recv_sems.at[11])
    chunk = z_in[0]
    for w in range(1, N_Z):
        chunk += z_in[w]
    last_in[pl.ds(x, 1)] = chunk[None]
    loop(1, N_X, lambda j: remote(last_in.at[x], last_in.at[x], 12, x_device(lax.rem(x + j, N_X))).start())
    wait_all(last_in.at[pl.ds(0, N_X - 1)], recv_sems.at[12])
    whole = jnp.concatenate(
        [jnp.concatenate([last_in[0], last_in[1]], axis=1), jnp.concatenate([last_in[2], last_in[3]], axis=1)], axis=0
    )
    grad_weight[...] = jnp.transpose(whole)

    wait_all(hub_z.at[pl.ds(0, N_Z - 1)], send_sems.at[0])
    wait_all(border_in.at[pl.ds(0, N_DOM - 1)], send_sems.at[1])
    wait_all(ints.at[pl.ds(0, N_FEAT - 1)], send_sems.at[2])
    wait_all(picked.at[0, pl.ds(0, N_FEAT - 1)], send_sems.at[3])
    wait_all(weight_t.at[pl.ds(0, N_FEAT - 1)], send_sems.at[4])
    wait_all(hub_x.at[pl.ds(0, N_X - 1)], send_sems.at[5])
    wait_all(picked.at[pl.ds(1, LIVE_FIRST - 1), pl.ds(0, N_FEAT - 1)], send_sems.at[6])
    wait_all(picked.at[pl.ds(LIVE_FIRST, SLOTS - LIVE_FIRST), pl.ds(0, N_FEAT - 1)], send_sems.at[7])
    to_core.wait_send()
    wait_all(y_in.at[pl.ds(0, N_Y - 1)], send_sems.at[9])
    wait_all(x_in.at[pl.ds(0, N_X - 1)], send_sems.at[10])
    wait_all(z_in.at[pl.ds(0, N_Z - 1)], send_sems.at[11])
    wait_all(last_in.at[pl.ds(0, N_X - 1)], send_sems.at[12])


def on_device(
    features, tile_vals, tile_src, tile_count, send_rows, hub_owner, hub_row, weight, cotangent
):
    vmem, smem = pl.BlockSpec(memory_space=pltpu.VMEM), pl.BlockSpec(memory_space=pltpu.SMEM)
    anywhere = pl.BlockSpec(memory_space=pl.ANY)
    scratch = [
        pltpu.VMEM(tile_vals.shape, F32),
        pltpu.VMEM(cotangent.shape, F32),
        pltpu.VMEM((EXT, SHARE, TILE), F32),
        pltpu.VMEM((N_FEAT, SLOTS, SHARE, TILE), F32),
        pltpu.VMEM((SLOTS, N_FEAT, SHARE, TILE), F32),
        pltpu.VMEM((N_FEAT, 1, TILE), I32),
        pltpu.SMEM((N_FEAT, 1, TILE), I32),
        pltpu.VMEM((N_DOM, 4, TILE), F32),
        pltpu.VMEM((N_DOM, 4, TILE), F32),
        pltpu.VMEM((8, TILE), F32),
        pltpu.VMEM((N_Z, 8, TILE), F32),
        pltpu.VMEM((N_X, N_Z, 8, TILE), F32),
        pltpu.VMEM((N_FEAT, SHARE, D), F32),
        pltpu.VMEM((2, N_Y, SHARE, D), F32),
        pltpu.VMEM((N_Y, SHARE, D), F32),
        pltpu.VMEM((N_Y, SHARE, D), F32),
        pltpu.VMEM((N_Y, SHARE, D), F32),
        pltpu.VMEM((N_X, 8, TILE), F32),
        pltpu.VMEM((N_X, 8, TILE), F32),
        pltpu.VMEM((8, TILE), F32),
        pltpu.VMEM((N_Z, 8, TILE), F32),
        pltpu.VMEM((N_X, 8, TILE), F32),
        pltpu.SemaphoreType.DMA((3,)),
        pltpu.SemaphoreType.DMA((13,)),
        pltpu.SemaphoreType.DMA((13,)),
    ]
    return pl.pallas_call(
        kernel,
        out_shape=(
            jax.ShapeDtypeStruct(cotangent.shape, F32),
            jax.ShapeDtypeStruct(weight.shape, F32),
        ),
        in_specs=[vmem, smem, smem, vmem, vmem, vmem, vmem, anywhere, anywhere],
        out_specs=(vmem, vmem),
        scratch_shapes=scratch,
        compiler_params=pltpu.CompilerParams(
            collective_id=0, has_side_effects=True, vmem_limit_bytes=40 * 1024 * 1024
        ),
    )(
        features, tile_src, tile_count, send_rows.reshape(BORDER, TILE),
        hub_owner.reshape(1, HUBS), hub_row.reshape(1, HUBS), weight, tile_vals, cotangent,
    )


def solution(mesh):
    in_specs = (
        P("feat", "dom"),
        P(("dom", "feat"), None, None, None),
        P(("dom", "feat"), None),
        P(("dom", "feat")),
        P("dom", None),
        P(),
        P(),
        P(None, "feat"),
        P(None, ("dom", "feat")),
    )
    out_specs = (P(None, ("dom", "feat")), P(None, "feat"))
    return jax.shard_map(
        on_device, mesh=mesh, in_specs=in_specs, out_specs=out_specs, check_vma=False
    )
```

time: 782 us -> 80.5 us (0.10)
  the two profiles are of different devices: /device:TPU:1 before, /device:TPU:2 now
where the time goes in v1:
time: 80.5 us; the launch traced here: 80.2 us
  Pallas kernels  73.2 us (91%)
  local copies, waits for them, and re-layouts  5.64 us (7%)
  between operations  1.36 us (2%)
    pallas_call x1, Pallas kernels, on_device(): pl.pallas_call(kernel, out_shape=(jax.ShapeDtypeStruct(cotangent.shape, F...  73.2 us
    unnamed x13, local copies, waits for them, and re-layouts  4.19 us

profile of v1, /device:TPU:2, one launch (start us, length us, event | category | flops | bytes accessed | tf_op | source)
XLA Modules:
  0.0 80.2 jit_solution(5418674388455077594)
XLA Ops:
  0.6 0.0 copy-start.4
  0.6 0.0 copy-start.1
  1.3 0.7 reshape.14.hub_owner
  2.0 0.0 copy-done.4
  2.0 0.8 copy.14
  2.8 0.1 reshape.13.send_rows
  2.9 0.0 copy-start.3
  2.9 0.8 %copy.15.weight = f32[256,16]{1,0:T(8,128)S(1)} copy(f32[256,16]{0,1:T(8,128)} %param.16) | data formatting | bytes 32768 | tf_op args[7]
  3.7 0.0 copy-done.1
  3.7 0.0 copy-done.3
  3.8 0.0 copy-start
  3.8 1.0 %copy-done = f32[1,6,128,128]{3,2,1,0:T(8,128)S(1)} copy-done((f32[1,6,128,128]{3,2,1,0:T(8,128)S(1)}, f32[1,6,128,128]{3,2,1,0:T(8,128)}, u32[]{:S(2)}) %copy-start) | copy-done | bytes 393240
  4.8 0.0 copy-start.2
  4.8 0.9 %copy-done.2 = f32[256,128]{1,0:T(8,128)S(1)} copy-done((f32[256,128]{1,0:T(8,128)S(1)}, f32[256,128]{1,0:T(8,128)}, u32[]{:S(2)}) %copy-start.2) | copy-done | bytes 131096
  5.7 73.2 %shard_map.104 = (f32[256,128]{1,0:T(8,128)S(1)}, f32[256,16]{1,0:T(8,128)S(1)}) custom-call(f32[16,2048]{1,0:T(8,128)S(1)} %copy-done.1, s32[1,6]{1,0:T(1,128)S(1)} %copy-done.3, s32[1]{0:T(128)S(6)} %copy.18.tile_count, s32[12,128]{1,0:T(8,128)S(1)} %reshape.13.send_rows, s32[1,768]{1,0:T(1,128)S(1)} %reshape.14.hub_owner, s32[1,768]{1,0:T(1,128)S(1)} %reshape.15.hub_row, ...), custom_call_target="tpu_custom_call" | custom-call | tf_op jit(solution)/shard_map/pallas_call | solution.py:343
  78.9 0.7 copy.16
  79.5 0.7 copy.19
  (1 shorter events, 0.0 us)
Async XLA Ops:
  0.6 1.4 %copy-start.4 = (s32[768]{0:T(1024)S(1)}, s32[768]{0:T(1024)}, u32[]{:S(2)}) copy-start(s32[768]{0:T(1024)} %param.15) | copy-start | bytes 9220
  0.6 3.1 %copy-start.1 = (f32[16,2048]{1,0:T(8,128)S(1)}, f32[16,2048]{1,0:T(8,128)}, u32[]{:S(2)}) copy-start(f32[16,2048]{1,0:T(8,128)} %features.1) | copy-start | bytes 393220
  2.9 0.8 %copy-start.3 = (s32[1,6]{1,0:T(1,128)S(1)}, s32[1,6]{1,0:T(1,128)}, u32[]{:S(2)}) copy-start(s32[1,6]{1,0:T(1,128)} %tile_src.1) | copy-start | bytes 76
  3.8 1.0 %copy-start = (f32[1,6,128,128]{3,2,1,0:T(8,128)S(1)}, f32[1,6,128,128]{3,2,1,0:T(8,128)}, u32[]{:S(2)}) copy-start(f32[1,6,128,128]{3,2,1,0:T(8,128)} %tile_vals.1) | copy-start | bytes 1179652
  4.8 0.9 %copy-start.2 = (f32[256,128]{1,0:T(8,128)S(1)}, f32[256,128]{1,0:T(8,128)}, u32[]{:S(2)}) copy-start(f32[256,128]{1,0:T(8,128)} %cotangent.1) | copy-start | bytes 393220

commit v2 on v1

v2 whole, which is shorter than its diff:
```python
import jax
import jax.numpy as jnp
from jax import lax
from jax.experimental import pallas as pl
from jax.experimental.pallas import tpu as pltpu
from jax.sharding import PartitionSpec as P

N_X, N_Z, N_Y = 4, 12, 8
N_DOM = N_X * N_Z
N_FEAT = 2 * N_Y
D = 256
TILE = 128
SHARE = D // N_FEAT
SEND = 32
SLOTS = 6
OWN = 16
BORDER = 12
HUB_TILES = 6
HUBS = HUB_TILES * TILE
EXT = OWN + BORDER + HUB_TILES
F32, BF16, I32 = jnp.float32, jnp.bfloat16, jnp.int32


def split(value):
    high = value.astype(BF16)
    return high, (value - high.astype(F32)).astype(BF16)


def dot3(a, b, dims):
    a_high, a_low = split(a)
    b_high, b_low = split(b)

    def one(u, v):
        return lax.dot_general(u, v, (dims, ((), ())), preferred_element_type=F32)

    return one(a_high, b_high) + (one(a_high, b_low) + one(a_low, b_high))


def pick(table, index):
    return jnp.take_along_axis(table, index, axis=1, mode="promise_in_bounds")


def loop(first, last, body):
    def step(i, carry):
        body(i)
        return carry

    lax.fori_loop(first, last, step, 0)


def far_first(i, n):
    return n // 2 + (i % 2) * ((i + 1) // 2) - (1 - i % 2) * (i // 2)


def each_dom(body):
    def of_z(i):
        for dx in (2, 1, 3, 0):
            body(i, dx)

    loop(0, N_Z - 1, of_z)
    for dx in (2, 1, 3):
        body(N_Z - 1, dx)


def kernel(
    tile_src, tile_count_hbm, features_hbm, send_rows_hbm, hub_owner_hbm, hub_row_hbm, weight_hbm, tile_vals, cotangent,
    output_hbm, grad_hbm,
    output, grad_weight, tile_count, features, send_rows, hub_owner, hub_row, row_list, vals, cot, source, stage, picked, ints, ints_smem,
    border_out, border_in, hub_out, hub_z, hub_part, hub_x, weight_t,
    core_out, core_in, y_out, y_in, sized, z_out, z_in, last_in,
    local_sems, send_sems, recv_sems,
):
    dom, feat = lax.axis_index("dom"), lax.axis_index("feat")
    z, x = dom // N_X, dom % N_X
    y, core = feat // 2, feat % 2

    def dom_far(i, dx):
        return lax.rem(z + far_first(i, N_Z), N_Z) * N_X + lax.rem(x + dx, N_X)

    def feat_far(i):
        t = N_FEAT - 2 - i
        j = (1 - t % 2) * (t // 2 + 1) + (t % 2) * (N_FEAT - 1 - t // 2)
        return lax.rem(feat + j, N_FEAT)

    def remote(src, dst, which, device):
        return pltpu.make_async_remote_copy(
            src_ref=src, dst_ref=dst, send_sem=send_sems.at[which], recv_sem=recv_sems.at[which],
            device_id=device, device_id_type=pl.DeviceIdType.MESH,
        )

    def wait_all(ref, sem):
        pltpu.make_async_copy(ref, ref, sem).wait()

    def wait_most(ref, sem):
        flat = sized.at[pl.ds(0, N_Y * N_X - 1)]
        wait_all(flat, sem)

    def fetch(src, dst, which):
        copy = pltpu.make_async_copy(src, dst, local_sems.at[which])
        copy.start()
        return copy

    barrier = pltpu.get_barrier_semaphore()
    each_dom(lambda i, dx: pl.semaphore_signal(
        barrier, inc=1, device_id={"dom": dom_far(i, dx)}, device_id_type=pl.DeviceIdType.MESH))
    loop(0, N_FEAT - 1, lambda i: pl.semaphore_signal(
        barrier, inc=1, device_id={"feat": feat_far(i)}, device_id_type=pl.DeviceIdType.MESH))

    owner_copy = fetch(hub_owner_hbm, hub_owner, 5)
    hub_row_copy = fetch(hub_row_hbm, hub_row, 6)
    features_copy = fetch(features_hbm, features, 3)
    rows_copy = fetch(send_rows_hbm, send_rows, 4)
    weight_copy = fetch(weight_hbm, weight_t.at[y, core], 7)
    count_copy = fetch(tile_count_hbm, tile_count, 8)
    vals_copy = fetch(tile_vals, vals, 0)
    cot_copy = fetch(cotangent, cot, 1)

    lane8 = lax.broadcasted_iota(I32, (8, TILE), 1)
    row8 = lax.broadcasted_iota(I32, (8, TILE), 0)

    features_copy.wait()
    for t in range(OWN):
        source[t] = features[:, t * TILE : (t + 1) * TILE]
    lane1 = lax.broadcasted_iota(I32, (1, TILE), 1)
    listed = jnp.zeros((1, TILE), I32)
    for k in range(SLOTS):
        listed = jnp.where(lane1 == k, tile_src[0, k], listed)
    ints[pl.ds(feat, 1)] = listed[None]

    owner_copy.wait()
    hub_row_copy.wait()
    owner = hub_owner[...].reshape(1, HUBS)
    earlier = (lax.broadcasted_iota(I32, (HUBS, HUBS), 0) < lax.broadcasted_iota(I32, (HUBS, HUBS), 1))
    owned = (lax.broadcasted_iota(I32, (N_DOM, HUBS), 0) == owner).astype(F32)
    before = jnp.dot(owned.astype(BF16), earlier.astype(F32).astype(BF16), preferred_element_type=F32)
    rank = jnp.dot(jnp.ones((8, N_DOM), BF16), (owned * before).astype(BF16), preferred_element_type=F32)
    rank = rank.astype(I32)
    mine = owner == dom
    place = lax.broadcasted_iota(I32, (TILE, HUBS), 0) % 64
    chosen = (mine & (rank[0:1] == place)).astype(F32).astype(BF16)
    row = hub_row[...].reshape(1, HUBS)
    row_parts = jnp.concatenate([jnp.broadcast_to(row // 16, (8, HUBS)), jnp.broadcast_to(row % 16, (8, HUBS))], axis=0)
    my_rows = lax.dot_general(
        row_parts.astype(F32).astype(BF16), chosen, (((1,), (1,)), ((), ())), preferred_element_type=F32
    )
    my_rows = my_rows[0:8].astype(I32) * 16 + my_rows[8:16].astype(I32)

    def columns(v, index):
        low, high = index % TILE, index // TILE
        found = jnp.zeros((8, TILE), F32)
        for t in range(OWN):
            part = pick(features[8 * v : 8 * v + 8, t * TILE : (t + 1) * TILE], low)
            found = jnp.where(high == t, part, found)
        return found

    hub_out[...] = jnp.where(lane8 < 64, columns(0, my_rows), columns(1, my_rows))

    rows_copy.wait()
    repeat = lax.broadcasted_iota(I32, (SEND, TILE), 1) % SEND == lax.broadcasted_iota(I32, (SEND, TILE), 0)
    row_list[...] = lax.dot_general(
        send_rows[...].astype(F32), repeat.astype(F32), (((0,), (0,)), ((), ())),
        precision=lax.Precision.HIGHEST, preferred_element_type=F32,
    ).astype(I32)

    group4 = lax.broadcasted_iota(I32, (4, TILE), 1) // 32
    in_group = [group4 == (t + x) % 4 for t in range(4)]

    def border_tile(q):
        lists = [jnp.broadcast_to(row_list[pl.ds(4 * q + d, 1), :], (8, TILE)) for d in range(4)]
        quarter = []
        for v in range(2):
            turned = lists[0]
            for d in range(1, 4):
                turned = jnp.where(lane8 // 32 == (d + 2 * v + row8 // 4 + x) % 4, lists[d], turned)
            found = columns(v, turned)
            quarter += [found[0:4], found[4:8]]
        for d in range(4):
            message = quarter[0]
            for a in range(4):
                message = jnp.where(in_group[(a + d) % 4], quarter[a], message)
            border_out[pl.ds(4 * q + d, 1)] = message[None]

    loop(0, BORDER, border_tile)

    weight_copy.wait()
    pl.semaphore_wait(barrier, N_DOM - 1 + N_FEAT - 1)

    def z_device(z_to):
        return {"dom": z_to * N_X + x}

    def x_device(x_to):
        return {"dom": z * N_X + x_to}

    def y_device(y_to):
        return {"feat": y_to * 2 + core}

    loop(0, N_Z - 1, lambda i: remote(
        hub_out, hub_z.at[z], 0, z_device(lax.rem(z + far_first(i, N_Z), N_Z))).start())
    each_dom(lambda i, dx: remote(
        border_out.at[dom_far(i, dx)], border_in.at[dom], 1, {"dom": dom_far(i, dx)}).start())
    loop(0, N_FEAT - 1, lambda i: remote(ints.at[feat], ints.at[feat], 2, {"feat": feat_far(i)}).start())
    loop(0, N_FEAT - 1, lambda i: remote(
        source.at[feat_far(i)], picked.at[0, feat], 3, {"feat": feat_far(i)}).start())
    loop(0, N_Y - 1, lambda i: remote(
        weight_t.at[y, core], weight_t.at[y, core], 4, y_device(lax.rem(y + far_first(i, N_Y), N_Y))).start())

    picked[0, pl.ds(feat, 1)] = source[pl.ds(feat, 1)]
    border_in[pl.ds(dom, 1)] = border_out[pl.ds(dom, 1)]
    hub_z[pl.ds(z, 1)] = hub_out[...][None]

    wait_all(hub_z.at[pl.ds(0, N_Z - 1)], recv_sems.at[0])
    owner8 = jnp.broadcast_to(owner, (8, HUBS))
    at = (owner8 // N_X % 2) * 64 + rank
    pair = jnp.where(owner8 % N_X == x, owner8 // (2 * N_X), N_Z)
    found = [jnp.zeros((8, TILE), F32)] * (2 * HUB_TILES)
    for p in range(N_Z // 2):
        even, odd = hub_z[2 * p], hub_z[2 * p + 1]
        tables = (
            jnp.where(lane8 < 64, even, pltpu.roll(odd, 64, 1)),
            jnp.where(lane8 < 64, pltpu.roll(even, 64, 1), odd),
        )
        for q in range(HUB_TILES):
            span = slice(q * TILE, (q + 1) * TILE)
            for v in range(2):
                found[2 * q + v] = jnp.where(pair[:, span] == p, pick(tables[v], at[:, span]), found[2 * q + v])
    for q in range(HUB_TILES):
        for v in range(2):
            hub_part[q, 8 * v : 8 * v + 8] = found[2 * q + v]
    loop(1, N_X, lambda j: remote(hub_part, hub_x.at[x], 5, x_device(lax.rem(x + j, N_X))).start())
    hub_x[pl.ds(x, 1)] = hub_part[...][None]

    wait_all(ints.at[pl.ds(0, N_FEAT - 1)], recv_sems.at[2])
    ints_copy = pltpu.make_async_copy(ints, ints_smem, local_sems.at[2])
    ints_copy.start()

    wait_all(border_in.at[pl.ds(0, N_DOM - 1)], recv_sems.at[1])
    quarter_of = [2 * v + row8 // 4 for v in range(2)]

    def border_arrived(q):
        pieces = []
        for e in range(4):
            piece = border_in[pl.ds(4 * q + e, 1)][0]
            pieces.append(jnp.concatenate([piece, piece], axis=0))
        for v in range(2):
            mixed = pieces[0]
            for e in range(1, 4):
                mixed = jnp.where(lane8 // 32 == (quarter_of[v] + e + x) % 4, pieces[e], mixed)
            source[pl.ds(OWN + q, 1), 8 * v : 8 * v + 8] = pick(mixed, (lane8 + 32 * (quarter_of[v] + x)) % TILE)[None]

    loop(0, BORDER, border_arrived)

    ints_copy.wait()

    def send_slots(first, last, which):
        def to_peer(i):
            peer = feat_far(i)
            for k in range(first, last):
                stage[peer, k] = source[ints_smem[peer, 0, k]]
            some = pl.ds(first, last - first)
            remote(stage.at[peer, some], picked.at[some, feat], which, {"feat": peer}).start()

        loop(0, N_FEAT - 1, to_peer)
        for k in range(first, last):
            picked[k, feat] = source[tile_src[0, k]]

    send_slots(1, 2, 6)
    wait_all(hub_x.at[pl.ds(0, N_X - 1)], recv_sems.at[5])
    for q in range(HUB_TILES):
        source[OWN + BORDER + q] = (hub_x[0, q] + hub_x[1, q]) + (hub_x[2, q] + hub_x[3, q])
    send_slots(2, 4, 7)
    send_slots(4, SLOTS, 10)
    wait_all(weight_t.at[pl.ds(0, N_Y - 1), 0], recv_sems.at[4])
    other = 1 - core
    weight_on = remote(weight_t.at[:, core], weight_t.at[:, core], 12, {"feat": y * 2 + other})
    weight_on.start()

    vals_copy.wait()
    count_copy.wait()
    count = tile_count[0]

    def aggregate(k):
        live = jnp.where(k < count, 1.0, 0.0).astype(F32)
        return dot3(picked[k].reshape(D, TILE), vals[0, k] * live, ((1,), (0,)))

    def arrived(first, last, which):
        wait_all(picked.at[pl.ds(first, last - first), pl.ds(0, N_FEAT - 1)], recv_sems.at[which])

    arrived(0, 1, 3)
    aggregated = aggregate(0)
    for first, last, which in ((1, 2, 6), (2, 4, 7), (4, SLOTS, 10)):
        if last == SLOTS:
            weight_on.wait_recv()
            cot_copy.wait()
        arrived(first, last, which)
        for k in range(first, last):
            aggregated += aggregate(k)

    result = jnp.tanh(dot3(weight_t[...].reshape(D, D), aggregated, ((1,), (0,))))
    output[...] = result
    output_copy = fetch(output, output_hbm, 9)
    pre_grad = cot[...] * (1.0 - result * result)
    partial = dot3(pre_grad, aggregated, ((1,), (1,)))

    for c in range(2):
        for w in range(N_Y):
            for j in range(N_X):
                top, left = SHARE * (2 * w + c) + 8 * (j // 2), TILE * (j % 2)
                core_out[c, w, j] = partial[top : top + 8, left : left + TILE]
    to_core = remote(core_out.at[other], core_in, 8, {"feat": y * 2 + other})
    to_core.start()
    to_core.wait_recv()
    y_out[...] = core_out[core] + core_in[...]

    def to_column(i, dx):
        y_to, x_to = lax.rem(y + far_first(i, N_Y), N_Y), lax.rem(x + dx, N_X)
        device = {"dom": z * N_X + x_to, "feat": y_to * 2 + core}
        remote(y_out.at[y_to, x_to], y_in.at[y, x], 9, device).start()

    def of_y(i):
        for dx in (2, 1, 3, 0):
            to_column(i, dx)

    loop(0, N_Y - 1, of_y)
    for dx in (2, 1, 3):
        to_column(N_Y - 1, dx)
    y_in[pl.ds(y, 1), pl.ds(x, 1)] = y_out[pl.ds(y, 1), pl.ds(x, 1)]
    wait_most(y_in, recv_sems.at[9])
    total = [y_in[w, 0] + y_in[w, 1] + (y_in[w, 2] + y_in[w, 3]) for w in range(N_Y)]
    while len(total) > 1:
        total = [a + b for a, b in zip(total[0::2], total[1::2])]
    z_out[...] = total[0]
    loop(0, N_Z - 1, lambda i: remote(
        z_out, z_in.at[z], 11, z_device(lax.rem(z + far_first(i, N_Z), N_Z))).start())
    z_in[pl.ds(z, 1)] = z_out[...][None]
    wait_all(z_in.at[pl.ds(0, N_Z - 1)], recv_sems.at[11])
    thirds = [z_in[w] + z_in[w + 1] + (z_in[w + 2] + z_in[w + 3]) for w in range(0, N_Z, 4)]
    chunk = thirds[0] + thirds[1] + thirds[2]
    last_in[pl.ds(x, 1)] = chunk[None]
    loop(1, N_X, lambda j: remote(last_in.at[x], last_in.at[x], 13, x_device(lax.rem(x + j, N_X))).start())
    wait_all(last_in.at[pl.ds(0, N_X - 1)], recv_sems.at[13])
    whole = jnp.concatenate(
        [jnp.concatenate([last_in[0], last_in[1]], axis=1), jnp.concatenate([last_in[2], last_in[3]], axis=1)], axis=0
    )
    grad_weight[...] = whole
    fetch(grad_weight, grad_hbm, 10).wait()
    output_copy.wait()

    wait_all(hub_z.at[pl.ds(0, N_Z - 1)], send_sems.at[0])
    wait_all(border_in.at[pl.ds(0, N_DOM - 1)], send_sems.at[1])
    wait_all(ints.at[pl.ds(0, N_FEAT - 1)], send_sems.at[2])
    wait_all(picked.at[0, pl.ds(0, N_FEAT - 1)], send_sems.at[3])
    wait_all(weight_t.at[pl.ds(0, N_Y - 1), 0], send_sems.at[4])
    wait_all(hub_x.at[pl.ds(0, N_X - 1)], send_sems.at[5])
    for first, last, which in ((1, 2, 6), (2, 4, 7), (4, SLOTS, 10)):
        wait_all(picked.at[pl.ds(first, last - first), pl.ds(0, N_FEAT - 1)], send_sems.at[which])
    weight_on.wait_send()
    to_core.wait_send()
    wait_most(y_in, send_sems.at[9])
    wait_all(z_in.at[pl.ds(0, N_Z - 1)], send_sems.at[11])
    wait_all(last_in.at[pl.ds(0, N_X - 1)], send_sems.at[13])


def hand_on(output, grad_weight, output_to, grad_to, sems):
    copies = (
        pltpu.make_async_copy(output, output_to, sems.at[0]),
        pltpu.make_async_copy(grad_weight, grad_to, sems.at[1]),
    )
    for copy in copies:
        copy.start()
    for copy in copies:
        copy.wait()


def on_device(
    features, tile_vals, tile_src, tile_count, send_rows, hub_owner, hub_row, weight, cotangent
):
    smem = pl.BlockSpec(memory_space=pltpu.SMEM)
    hbm = pl.BlockSpec(memory_space=pltpu.HBM)
    scratch = [
        pltpu.VMEM(cotangent.shape, F32),
        pltpu.VMEM((SHARE, D), F32),
        pltpu.SMEM(tile_count.shape, I32),
        pltpu.VMEM(features.shape, F32),
        pltpu.VMEM((SEND, N_DOM), I32),
        pltpu.VMEM((HUBS,), I32),
        pltpu.VMEM((HUBS,), I32),
        pltpu.VMEM((N_DOM, TILE), I32),
        pltpu.VMEM(tile_vals.shape, F32),
        pltpu.VMEM(cotangent.shape, F32),
        pltpu.VMEM((EXT, SHARE, TILE), F32),
        pltpu.VMEM((N_FEAT, SLOTS, SHARE, TILE), F32),
        pltpu.VMEM((SLOTS, N_FEAT, SHARE, TILE), F32),
        pltpu.VMEM((N_FEAT, 1, TILE), I32),
        pltpu.SMEM((N_FEAT, 1, TILE), I32),
        pltpu.VMEM((N_DOM, 4, TILE), F32),
        pltpu.VMEM((N_DOM, 4, TILE), F32),
        pltpu.VMEM((8, TILE), F32),
        pltpu.VMEM((N_Z, 8, TILE), F32),
        pltpu.VMEM((HUB_TILES, SHARE, TILE), F32),
        pltpu.VMEM((N_X, HUB_TILES, SHARE, TILE), F32),
        pltpu.VMEM((N_Y, 2, SHARE, D), F32),
        pltpu.VMEM((2, N_Y, N_X, 8, TILE), F32),
        pltpu.VMEM((N_Y, N_X, 8, TILE), F32),
        pltpu.VMEM((N_Y, N_X, 8, TILE), F32),
        pltpu.VMEM((N_Y, N_X, 8, TILE), F32),
        pltpu.VMEM((N_Y * N_X, 8, TILE), F32),
        pltpu.VMEM((8, TILE), F32),
        pltpu.VMEM((N_Z, 8, TILE), F32),
        pltpu.VMEM((N_X, 8, TILE), F32),
        pltpu.SemaphoreType.DMA((11,)),
        pltpu.SemaphoreType.DMA((14,)),
        pltpu.SemaphoreType.DMA((14,)),
    ]
    results = (
        jax.ShapeDtypeStruct(cotangent.shape, F32),
        jax.ShapeDtypeStruct((SHARE, D), F32),
    )
    made = pl.pallas_call(
        kernel,
        out_shape=results,
        in_specs=[smem] + [hbm] * 8,
        out_specs=(hbm, hbm),
        scratch_shapes=scratch,
        compiler_params=pltpu.CompilerParams(
            collective_id=0, has_side_effects=True, vmem_limit_bytes=60 * 1024 * 1024
        ),
    )(
        tile_src, tile_count, features, send_rows.T, hub_owner, hub_row, weight.T, tile_vals, cotangent
    )
    output, grad_weight = pl.pallas_call(
        hand_on,
        out_shape=results,
        in_specs=[hbm, hbm],
        out_specs=(hbm, hbm),
        scratch_shapes=[pltpu.SemaphoreType.DMA((2,))],
        compiler_params=pltpu.CompilerParams(vmem_limit_bytes=60 * 1024 * 1024),
    )(*made)
    return output, grad_weight.T


def solution(mesh):
    in_specs = (
        P("feat", "dom"),
        P(("dom", "feat"), None, None, None),
        P(("dom", "feat"), None),
        P(("dom", "feat")),
        P("dom", None),
        P(),
        P(),
        P(None, "feat"),
        P(None, ("dom", "feat")),
    )
    out_specs = (P(None, ("dom", "feat")), P(None, "feat"))
    return jax.shard_map(
        on_device, mesh=mesh, in_specs=in_specs, out_specs=out_specs, check_vma=False
    )
```

time: 80.5 us -> 71.7 us (0.89)
  the two profiles are of different devices: /device:TPU:2 before, /device:TPU:1 now
where the time goes in v2:
time: 71.7 us; the launch traced here: 71.5 us
  Pallas kernels  70.2 us (98%)
  between operations  1.29 us (2%)
    pallas_call x1, Pallas kernels, on_device(): pl.pallas_call(kernel, out_shape=results, in_specs=[smem] + [hbm] * 8, ou...  64.6 us
    pallas_call x1, Pallas kernels, on_device(): pl.pallas_call(hand_on, out_shape=results, in_specs=[hbm, hbm], out_specs...  5.59 us

profile of v2, /device:TPU:1, one launch (start us, length us, event | category | flops | bytes accessed | tf_op | source)
XLA Modules:
  0.0 71.5 jit_solution(5586139393134352356)
XLA Ops:
  1.3 64.6 %shard_map.104 = (f32[256,128]{1,0:T(8,128)}, f32[16,256]{1,0:T(8,128)}) custom-call(s32[1,6]{1,0:T(1,128)} %tile_src.1, s32[1]{0:T(128)S(6)} %copy.11.tile_count_hbm, f32[16,2048]{1,0:T(8,128)} %features_hbm.1, s32[32,48]{1,0:T(8,128)} %bitcast.3, s32[768]{0:T(1024)} %hub_owner_hbm.1, s32[768]{0:T(1024)} %hub_row_hbm.1, f32[16,256]{1,0:T(8,128)} %bitcast.4, ...), custom_call_target="tpu_custom_call" | custom-call | tf_op jit(solution)/shard_map/pallas_call | solution.py:418
  65.9 5.6 %shard_map.105 = (f32[256,128]{1,0:T(8,128)}, f32[16,256]{1,0:T(8,128)}) custom-call(f32[256,128]{1,0:T(8,128)} %get-tuple-element.6.output, f32[16,256]{1,0:T(8,128)} %get-tuple-element.7.grad_weight), custom_call_target="tpu_custom_call" | custom-call | tf_op jit(solution)/shard_map/pallas_call | solution.py:430

commit v3 on v2

--- a/solution.py
+++ b/solution.py
@@ -360,14 +360,16 @@
     wait_all(last_in.at[pl.ds(0, N_X - 1)], send_sems.at[13])
 
 
-def hand_on(output, grad_weight, output_to, grad_to, sems):
-    copies = (
-        pltpu.make_async_copy(output, output_to, sems.at[0]),
-        pltpu.make_async_copy(grad_weight, grad_to, sems.at[1]),
-    )
-    for copy in copies:
+def hand_on(output, grad_weight, output_to, grad_to, held, held_grad, sems):
+    ways = ((output, held, output_to), (grad_weight, held_grad, grad_to))
+    incoming = [pltpu.make_async_copy(w[0], w[1], sems.at[i]) for i, w in enumerate(ways)]
+    outgoing = [pltpu.make_async_copy(w[1], w[2], sems.at[2 + i]) for i, w in enumerate(ways)]
+    for copy in incoming:
         copy.start()
-    for copy in copies:
+    for copy, onward in zip(incoming, outgoing):
+        copy.wait()
+        onward.start()
+    for copy in outgoing:
         copy.wait()
 
 
@@ -432,7 +434,7 @@
         out_shape=results,
         in_specs=[hbm, hbm],
         out_specs=(hbm, hbm),
-        scratch_shapes=[pltpu.SemaphoreType.DMA((2,))],
+        scratch_shapes=[pltpu.VMEM(r.shape, F32) for r in results] + [pltpu.SemaphoreType.DMA((4,))],
         compiler_params=pltpu.CompilerParams(vmem_limit_bytes=60 * 1024 * 1024),
     )(*made)
     return output, grad_weight.T

time: 71.7 us -> 67.7 us (0.944)
  Pallas kernels: 70.2 us -> 66.2 us
    pallas_call x1, Pallas kernels: 5.59 us -> 1.6 us  [on_device(): pl.pallas_call(hand_on, out_shape=results, in_specs=[hbm, hbm], out_specs...]
where the time goes in v3:
time: 67.7 us; the launch traced here: 67.5 us
  Pallas kernels  66.2 us (98%)
  between operations  1.29 us (2%)
    pallas_call x1, Pallas kernels, on_device(): pl.pallas_call(kernel, out_shape=results, in_specs=[smem] + [hbm] * 8, ou...  64.6 us
    pallas_call x1, Pallas kernels, on_device(): pl.pallas_call(hand_on, out_shape=results, in_specs=[hbm, hbm], out_specs...  1.6 us

profile of v3, /device:TPU:1, one launch (start us, length us, event | category | flops | bytes accessed | tf_op | source)
XLA Modules:
  0.0 67.5 jit_solution(8797312071926778908)
XLA Ops:
  1.3 64.6 %shard_map.104 = (f32[256,128]{1,0:T(8,128)}, f32[16,256]{1,0:T(8,128)}) custom-call(s32[1,6]{1,0:T(1,128)} %tile_src.1, s32[1]{0:T(128)S(6)} %copy.11.tile_count_hbm, f32[16,2048]{1,0:T(8,128)} %features_hbm.1, s32[32,48]{1,0:T(8,128)} %bitcast.3, s32[768]{0:T(1024)} %hub_owner_hbm.1, s32[768]{0:T(1024)} %hub_row_hbm.1, f32[16,256]{1,0:T(8,128)} %bitcast.4, ...), custom_call_target="tpu_custom_call" | custom-call | tf_op jit(solution)/shard_map/pallas_call | solution.py:420
  65.9 1.6 %shard_map.105 = (f32[256,128]{1,0:T(8,128)}, f32[16,256]{1,0:T(8,128)}) custom-call(f32[256,128]{1,0:T(8,128)} %get-tuple-element.6.output, f32[16,256]{1,0:T(8,128)} %get-tuple-element.7.grad_weight), custom_call_target="tpu_custom_call" | custom-call | tf_op jit(solution)/shard_map/pallas_call | solution.py:432

commit v4 on v3

--- a/solution.py
+++ b/solution.py
@@ -26,14 +26,11 @@
     return high, (value - high.astype(F32)).astype(BF16)
 
 
-def dot3(a, b, dims):
-    a_high, a_low = split(a)
-    b_high, b_low = split(b)
-
+def product(a, b, dims):
     def one(u, v):
         return lax.dot_general(u, v, (dims, ((), ())), preferred_element_type=F32)
 
-    return one(a_high, b_high) + (one(a_high, b_low) + one(a_low, b_high))
+    return one(a[0], b[0]) + (one(a[0], b[1]) + one(a[1], b[0]))
 
 
 def pick(table, index):
@@ -63,9 +60,9 @@
 
 
 def kernel(
-    tile_src, tile_count_hbm, features_hbm, send_rows_hbm, hub_owner_hbm, hub_row_hbm, weight_hbm, tile_vals, cotangent,
+    tile_src_hbm, tile_count_hbm, features_hbm, send_rows_hbm, hub_owner_hbm, hub_row_hbm, weight_hbm, tile_vals, cotangent,
     output_hbm, grad_hbm,
-    output, grad_weight, tile_count, features, send_rows, hub_owner, hub_row, row_list, vals, cot, source, stage, picked, ints, ints_smem,
+    output, grad_weight, tile_src, tile_count, features, send_rows, hub_owner, hub_row, row_list, vals, vals_high, vals_low, cot, pre_grad, source, stage, picked, ints, ints_smem,
     border_out, border_in, hub_out, hub_z, hub_part, hub_x, weight_t,
     core_out, core_in, y_out, y_in, sized, z_out, z_in, last_in,
     local_sems, send_sems, recv_sems,
@@ -106,6 +103,7 @@
     loop(0, N_FEAT - 1, lambda i: pl.semaphore_signal(
         barrier, inc=1, device_id={"feat": feat_far(i)}, device_id_type=pl.DeviceIdType.MESH))
 
+    src_copy = fetch(tile_src_hbm, tile_src, 11)
     owner_copy = fetch(hub_owner_hbm, hub_owner, 5)
     hub_row_copy = fetch(hub_row_hbm, hub_row, 6)
     features_copy = fetch(features_hbm, features, 3)
@@ -119,14 +117,64 @@
     row8 = lax.broadcasted_iota(I32, (8, TILE), 0)
 
     features_copy.wait()
+    def columns(v, index):
+        low, high = index % TILE, index // TILE
+        found = jnp.zeros((8, TILE), F32)
+        for t in range(OWN):
+            part = pick(features[8 * v : 8 * v + 8, t * TILE : (t + 1) * TILE], low)
+            found = jnp.where(high == t, part, found)
+        return found
+
+    rows_copy.wait()
+    repeat = lax.broadcasted_iota(I32, (SEND, TILE), 1) % SEND == lax.broadcasted_iota(I32, (SEND, TILE), 0)
+    row_list[...] = lax.dot_general(
+        send_rows[...].astype(F32), repeat.astype(F32), (((0,), (0,)), ((), ())),
+        precision=lax.Precision.HIGHEST, preferred_element_type=F32,
+    ).astype(I32)
+
+    group4 = lax.broadcasted_iota(I32, (4, TILE), 1) // 32
+    in_group = [group4 == (t + x) % 4 for t in range(4)]
+
+    def border_tile(q):
+        lists = [jnp.broadcast_to(row_list[pl.ds(4 * q + d, 1), :], (8, TILE)) for d in range(4)]
+        quarter = []
+        for v in range(2):
+            turned = lists[0]
+            for d in range(1, 4):
+                turned = jnp.where(lane8 // 32 == (d + 2 * v + row8 // 4 + x) % 4, lists[d], turned)
+            found = columns(v, turned)
+            quarter += [found[0:4], found[4:8]]
+        for d in range(4):
+            message = quarter[0]
+            for a in range(4):
+                message = jnp.where(in_group[(a + d) % 4], quarter[a], message)
+            border_out[pl.ds(4 * q + d, 1)] = message[None]
+
+    loop(0, BORDER, border_tile)
+
     for t in range(OWN):
         source[t] = features[:, t * TILE : (t + 1) * TILE]
     lane1 = lax.broadcasted_iota(I32, (1, TILE), 1)
+    src_copy.wait()
     listed = jnp.zeros((1, TILE), I32)
     for k in range(SLOTS):
         listed = jnp.where(lane1 == k, tile_src[0, k], listed)
     ints[pl.ds(feat, 1)] = listed[None]
 
+    weight_copy.wait()
+    pl.semaphore_wait(barrier, N_DOM - 1 + N_FEAT - 1)
+
+    def z_device(z_to):
+        return {"dom": z_to * N_X + x}
+
+    def x_device(x_to):
+        return {"dom": z * N_X + x_to}
+
+    def y_device(y_to):
+        return {"feat": y_to * 2 + core}
+
+    each_dom(lambda i, dx: remote(
+        border_out.at[dom_far(i, dx)], border_in.at[dom], 1, {"dom": dom_far(i, dx)}).start())
     owner_copy.wait()
     hub_row_copy.wait()
     owner = hub_owner[...].reshape(1, HUBS)
@@ -145,59 +193,10 @@
     )
     my_rows = my_rows[0:8].astype(I32) * 16 + my_rows[8:16].astype(I32)
 
-    def columns(v, index):
-        low, high = index % TILE, index // TILE
-        found = jnp.zeros((8, TILE), F32)
-        for t in range(OWN):
-            part = pick(features[8 * v : 8 * v + 8, t * TILE : (t + 1) * TILE], low)
-            found = jnp.where(high == t, part, found)
-        return found
-
     hub_out[...] = jnp.where(lane8 < 64, columns(0, my_rows), columns(1, my_rows))
-
-    rows_copy.wait()
-    repeat = lax.broadcasted_iota(I32, (SEND, TILE), 1) % SEND == lax.broadcasted_iota(I32, (SEND, TILE), 0)
-    row_list[...] = lax.dot_general(
-        send_rows[...].astype(F32), repeat.astype(F32), (((0,), (0,)), ((), ())),
-        precision=lax.Precision.HIGHEST, preferred_element_type=F32,
-    ).astype(I32)
-
-    group4 = lax.broadcasted_iota(I32, (4, TILE), 1) // 32
-    in_group = [group4 == (t + x) % 4 for t in range(4)]
-
-    def border_tile(q):
-        lists = [jnp.broadcast_to(row_list[pl.ds(4 * q + d, 1), :], (8, TILE)) for d in range(4)]
-        quarter = []
-        for v in range(2):
-            turned = lists[0]
-            for d in range(1, 4):
-                turned = jnp.where(lane8 // 32 == (d + 2 * v + row8 // 4 + x) % 4, lists[d], turned)
-            found = columns(v, turned)
-            quarter += [found[0:4], found[4:8]]
-        for d in range(4):
-            message = quarter[0]
-            for a in range(4):
-                message = jnp.where(in_group[(a + d) % 4], quarter[a], message)
-            border_out[pl.ds(4 * q + d, 1)] = message[None]
-
-    loop(0, BORDER, border_tile)
-
-    weight_copy.wait()
-    pl.semaphore_wait(barrier, N_DOM - 1 + N_FEAT - 1)
-
-    def z_device(z_to):
-        return {"dom": z_to * N_X + x}
-
-    def x_device(x_to):
-        return {"dom": z * N_X + x_to}
-
-    def y_device(y_to):
-        return {"feat": y_to * 2 + core}
 
     loop(0, N_Z - 1, lambda i: remote(
         hub_out, hub_z.at[z], 0, z_device(lax.rem(z + far_first(i, N_Z), N_Z))).start())
-    each_dom(lambda i, dx: remote(
-        border_out.at[dom_far(i, dx)], border_in.at[dom], 1, {"dom": dom_far(i, dx)}).start())
     loop(0, N_FEAT - 1, lambda i: remote(ints.at[feat], ints.at[feat], 2, {"feat": feat_far(i)}).start())
     loop(0, N_FEAT - 1, lambda i: remote(
         source.at[feat_far(i)], picked.at[0, feat], 3, {"feat": feat_far(i)}).start())
@@ -277,39 +276,44 @@
     vals_copy.wait()
     count_copy.wait()
     count = tile_count[0]
-
-    def aggregate(k):
+    for k in range(SLOTS):
         live = jnp.where(k < count, 1.0, 0.0).astype(F32)
-        return dot3(picked[k].reshape(D, TILE), vals[0, k] * live, ((1,), (0,)))
-
-    def arrived(first, last, which):
+        vals_high[k], vals_low[k] = split(vals[0, k] * live)
+
+    def aggregate(first, last, which):
         wait_all(picked.at[pl.ds(first, last - first), pl.ds(0, N_FEAT - 1)], recv_sems.at[which])
-
-    arrived(0, 1, 3)
-    aggregated = aggregate(0)
-    for first, last, which in ((1, 2, 6), (2, 4, 7), (4, SLOTS, 10)):
-        if last == SLOTS:
-            weight_on.wait_recv()
-            cot_copy.wait()
-        arrived(first, last, which)
-        for k in range(first, last):
-            aggregated += aggregate(k)
-
-    result = jnp.tanh(dot3(weight_t[...].reshape(D, D), aggregated, ((1,), (0,))))
+        taken = [picked[k].reshape(D, TILE) for k in range(first, last)]
+        taken = split(jnp.concatenate(taken, axis=1))
+        rows = (last - first) * TILE
+        factor = (vals_high[first:last].reshape(rows, TILE), vals_low[first:last].reshape(rows, TILE))
+        return product(taken, factor, ((1,), (0,)))
+
+    aggregated = aggregate(0, 1, 3)
+    aggregated += aggregate(1, 2, 6)
+    weight_on.wait_recv()
+    weight_parts = split(weight_t[...].reshape(D, D))
+    cot_copy.wait()
+    aggregated += aggregate(2, 4, 7)
+    aggregated += aggregate(4, SLOTS, 10)
+    parts = split(aggregated)
+    result = jnp.tanh(product(weight_parts, parts, ((1,), (0,))))
     output[...] = result
     output_copy = fetch(output, output_hbm, 9)
-    pre_grad = cot[...] * (1.0 - result * result)
-    partial = dot3(pre_grad, aggregated, ((1,), (1,)))
-
-    for c in range(2):
+    pre_grad[...] = (cot[...] * (1.0 - result * result)).reshape(pre_grad.shape)
+
+    def gradient(c, to):
+        partial = product(split(pre_grad[:, c].reshape(N_Y * SHARE, TILE)), parts, ((1,), (1,)))
         for w in range(N_Y):
             for j in range(N_X):
-                top, left = SHARE * (2 * w + c) + 8 * (j // 2), TILE * (j % 2)
-                core_out[c, w, j] = partial[top : top + 8, left : left + TILE]
-    to_core = remote(core_out.at[other], core_in, 8, {"feat": y * 2 + other})
+                top, left = SHARE * w + 8 * (j // 2), TILE * (j % 2)
+                to[w, j] = partial[top : top + 8, left : left + TILE]
+
+    gradient(other, core_out)
+    to_core = remote(core_out, core_in, 8, {"feat": y * 2 + other})
     to_core.start()
+    gradient(core, y_out)
     to_core.wait_recv()
-    y_out[...] = core_out[core] + core_in[...]
+    y_out[...] += core_in[...]
 
     def to_column(i, dx):
         y_to, x_to = lax.rem(y + far_first(i, N_Y), N_Y), lax.rem(x + dx, N_X)
@@ -376,11 +380,11 @@
 def on_device(
     features, tile_vals, tile_src, tile_count, send_rows, hub_owner, hub_row, weight, cotangent
 ):
-    smem = pl.BlockSpec(memory_space=pltpu.SMEM)
     hbm = pl.BlockSpec(memory_space=pltpu.HBM)
     scratch = [
         pltpu.VMEM(cotangent.shape, F32),
         pltpu.VMEM((SHARE, D), F32),
+        pltpu.SMEM(tile_src.shape, I32),
         pltpu.SMEM(tile_count.shape, I32),
         pltpu.VMEM(features.shape, F32),
         pltpu.VMEM((SEND, N_DOM), I32),
@@ -388,7 +392,10 @@
         pltpu.VMEM((HUBS,), I32),
         pltpu.VMEM((N_DOM, TILE), I32),
         pltpu.VMEM(tile_vals.shape, F32),
+        pltpu.VMEM((SLOTS, TILE, TILE), BF16),
+        pltpu.VMEM((SLOTS, TILE, TILE), BF16),
         pltpu.VMEM(cotangent.shape, F32),
+        pltpu.VMEM((N_Y, 2, SHARE, TILE), F32),
         pltpu.VMEM((EXT, SHARE, TILE), F32),
         pltpu.VMEM((N_FEAT, SLOTS, SHARE, TILE), F32),
         pltpu.VMEM((SLOTS, N_FEAT, SHARE, TILE), F32),
@@ -401,7 +408,7 @@
         pltpu.VMEM((HUB_TILES, SHARE, TILE), F32),
         pltpu.VMEM((N_X, HUB_TILES, SHARE, TILE), F32),
         pltpu.VMEM((N_Y, 2, SHARE, D), F32),
-        pltpu.VMEM((2, N_Y, N_X, 8, TILE), F32),
+        pltpu.VMEM((N_Y, N_X, 8, TILE), F32),
         pltpu.VMEM((N_Y, N_X, 8, TILE), F32),
         pltpu.VMEM((N_Y, N_X, 8, TILE), F32),
         pltpu.VMEM((N_Y, N_X, 8, TILE), F32),
@@ -409,7 +416,7 @@
         pltpu.VMEM((8, TILE), F32),
         pltpu.VMEM((N_Z, 8, TILE), F32),
         pltpu.VMEM((N_X, 8, TILE), F32),
-        pltpu.SemaphoreType.DMA((11,)),
+        pltpu.SemaphoreType.DMA((12,)),
         pltpu.SemaphoreType.DMA((14,)),
         pltpu.SemaphoreType.DMA((14,)),
     ]
@@ -420,7 +427,7 @@
     made = pl.pallas_call(
         kernel,
         out_shape=results,
-        in_specs=[smem] + [hbm] * 8,
+        in_specs=[hbm] * 9,
         out_specs=(hbm, hbm),
         scratch_shapes=scratch,
         compiler_params=pltpu.CompilerParams(

time: 67.7 us -> 66.7 us (0.985)
  Pallas kernels: 66.2 us -> 65 us
    pallas_call x1, Pallas kernels: 64.6 us -> 63.4 us  [on_device(): pl.pallas_call(kernel, out_shape=results, in_specs=[hbm] * 9, out_specs=(...]
where the time goes in v4:
time: 66.7 us; the launch traced here: 66.3 us
  Pallas kernels  65 us (97%)
  between operations  1.29 us (2%)
    pallas_call x1, Pallas kernels, on_device(): pl.pallas_call(kernel, out_shape=results, in_specs=[hbm] * 9, out_specs=(...  63.4 us
    pallas_call x1, Pallas kernels, on_device(): pl.pallas_call(hand_on, out_shape=results, in_specs=[hbm, hbm], out_specs...  1.6 us

profile of v4, /device:TPU:1, one launch (start us, length us, event | category | flops | bytes accessed | tf_op | source)
XLA Modules:
  0.0 66.3 jit_solution(2172340492974128779)
XLA Ops:
  1.3 63.4 %shard_map.104 = (f32[256,128]{1,0:T(8,128)}, f32[16,256]{1,0:T(8,128)}) custom-call(s32[1,6]{1,0:T(1,128)} %tile_src_hbm.1, s32[1]{0:T(128)S(6)} %copy.11.tile_count_hbm, f32[16,2048]{1,0:T(8,128)} %features_hbm.1, s32[32,48]{1,0:T(8,128)} %bitcast.3, s32[768]{0:T(1024)} %hub_owner_hbm.1, s32[768]{0:T(1024)} %hub_row_hbm.1, f32[16,256]{1,0:T(8,128)} %bitcast.4, ...), custom_call_target="tpu_custom_call" | custom-call | tf_op jit(solution)/shard_map/pallas_call | solution.py:427
  64.7 1.6 %shard_map.105 = (f32[256,128]{1,0:T(8,128)}, f32[16,256]{1,0:T(8,128)}) custom-call(f32[256,128]{1,0:T(8,128)} %get-tuple-element.6.output, f32[16,256]{1,0:T(8,128)} %get-tuple-element.7.grad_weight), custom_call_target="tpu_custom_call" | custom-call | tf_op jit(solution)/shard_map/pallas_call | solution.py:439

commit v5 on v4

--- a/solution.py
+++ b/solution.py
@@ -50,13 +50,13 @@
 
 
 def each_dom(body):
-    def of_z(i):
-        for dx in (2, 1, 3, 0):
-            body(i, dx)
-
-    loop(0, N_Z - 1, of_z)
-    for dx in (2, 1, 3):
-        body(N_Z - 1, dx)
+    def hops(at):
+        dz = far_first(at[0], N_Z)
+        return min(dz, N_Z - dz) + min(at[1], N_X - at[1])
+
+    offsets = [(i, dx) for i in range(N_Z) for dx in (2, 1, 3, 0)][:-1]
+    for i, dx in sorted(offsets, key=hops, reverse=True):
+        body(i, dx)
 
 
 def kernel(
@@ -320,13 +320,10 @@
         device = {"dom": z * N_X + x_to, "feat": y_to * 2 + core}
         remote(y_out.at[y_to, x_to], y_in.at[y, x], 9, device).start()
 
-    def of_y(i):
+    for i in range(N_Y):
         for dx in (2, 1, 3, 0):
-            to_column(i, dx)
-
-    loop(0, N_Y - 1, of_y)
-    for dx in (2, 1, 3):
-        to_column(N_Y - 1, dx)
+            if (i, dx) != (N_Y - 1, 0):
+                to_column(i, dx)
     y_in[pl.ds(y, 1), pl.ds(x, 1)] = y_out[pl.ds(y, 1), pl.ds(x, 1)]
     wait_most(y_in, recv_sems.at[9])
     total = [y_in[w, 0] + y_in[w, 1] + (y_in[w, 2] + y_in[w, 3]) for w in range(N_Y)]

time: 66.7 us -> 66.4 us (level)
  no operation moved by 1% of the time
where the time goes in v5:
time: 66.4 us; the launch traced here: 65.8 us
  Pallas kernels  64.5 us (97%)
  between operations  1.29 us (2%)
    pallas_call x1, Pallas kernels, on_device(): pl.pallas_call(kernel, out_shape=results, in_specs=[hbm] * 9, out_specs=(...  62.9 us
    pallas_call x1, Pallas kernels, on_device(): pl.pallas_call(hand_on, out_shape=results, in_specs=[hbm, hbm], out_specs...  1.6 us

profile of v5, /device:TPU:1, one launch (start us, length us, event | category | flops | bytes accessed | tf_op | source)
XLA Modules:
  0.0 65.8 jit_solution(9283450368878423207)
XLA Ops:
  1.3 62.9 %shard_map.104 = (f32[256,128]{1,0:T(8,128)}, f32[16,256]{1,0:T(8,128)}) custom-call(s32[1,6]{1,0:T(1,128)} %tile_src_hbm.1, s32[1]{0:T(128)S(6)} %copy.11.tile_count_hbm, f32[16,2048]{1,0:T(8,128)} %features_hbm.1, s32[32,48]{1,0:T(8,128)} %bitcast.3, s32[768]{0:T(1024)} %hub_owner_hbm.1, s32[768]{0:T(1024)} %hub_row_hbm.1, f32[16,256]{1,0:T(8,128)} %bitcast.4, ...), custom_call_target="tpu_custom_call" | custom-call | tf_op jit(solution)/shard_map/pallas_call | solution.py:424
  64.2 1.6 %shard_map.105 = (f32[256,128]{1,0:T(8,128)}, f32[16,256]{1,0:T(8,128)}) custom-call(f32[256,128]{1,0:T(8,128)} %get-tuple-element.6.output, f32[16,256]{1,0:T(8,128)} %get-tuple-element.7.grad_weight), custom_call_target="tpu_custom_call" | custom-call | tf_op jit(solution)/shard_map/pallas_call | solution.py:436

commit v6 on v5

--- a/solution.py
+++ b/solution.py
@@ -62,7 +62,7 @@
 def kernel(
     tile_src_hbm, tile_count_hbm, features_hbm, send_rows_hbm, hub_owner_hbm, hub_row_hbm, weight_hbm, tile_vals, cotangent,
     output_hbm, grad_hbm,
-    output, grad_weight, tile_src, tile_count, features, send_rows, hub_owner, hub_row, row_list, vals, vals_high, vals_low, cot, pre_grad, source, stage, picked, ints, ints_smem,
+    output, tile_src, tile_count, features, send_rows, hub_owner, hub_row, row_list, vals, vals_high, vals_low, cot, pre_grad, source, stage, picked, ints, ints_smem,
     border_out, border_in, hub_out, hub_z, hub_part, hub_x, weight_t,
     core_out, core_in, y_out, y_in, sized, z_out, z_in, last_in,
     local_sems, send_sems, recv_sems,
@@ -338,14 +338,6 @@
     chunk = thirds[0] + thirds[1] + thirds[2]
     last_in[pl.ds(x, 1)] = chunk[None]
     loop(1, N_X, lambda j: remote(last_in.at[x], last_in.at[x], 13, x_device(lax.rem(x + j, N_X))).start())
-    wait_all(last_in.at[pl.ds(0, N_X - 1)], recv_sems.at[13])
-    whole = jnp.concatenate(
-        [jnp.concatenate([last_in[0], last_in[1]], axis=1), jnp.concatenate([last_in[2], last_in[3]], axis=1)], axis=0
-    )
-    grad_weight[...] = whole
-    fetch(grad_weight, grad_hbm, 10).wait()
-    output_copy.wait()
-
     wait_all(hub_z.at[pl.ds(0, N_Z - 1)], send_sems.at[0])
     wait_all(border_in.at[pl.ds(0, N_DOM - 1)], send_sems.at[1])
     wait_all(ints.at[pl.ds(0, N_FEAT - 1)], send_sems.at[2])
@@ -358,7 +350,15 @@
     to_core.wait_send()
     wait_most(y_in, send_sems.at[9])
     wait_all(z_in.at[pl.ds(0, N_Z - 1)], send_sems.at[11])
+    output_copy.wait()
+    wait_all(last_in.at[pl.ds(0, N_X - 1)], recv_sems.at[13])
+    grad_copies = [
+        fetch(last_in.at[j], grad_hbm.at[pl.ds(8 * (j // 2), 8), pl.ds(TILE * (j % 2), TILE)], (10, 12, 13, 14)[j])
+        for j in range(N_X)
+    ]
     wait_all(last_in.at[pl.ds(0, N_X - 1)], send_sems.at[13])
+    for copy in grad_copies:
+        copy.wait()
 
 
 def hand_on(output, grad_weight, output_to, grad_to, held, held_grad, sems):
@@ -380,7 +380,6 @@
     hbm = pl.BlockSpec(memory_space=pltpu.HBM)
     scratch = [
         pltpu.VMEM(cotangent.shape, F32),
-        pltpu.VMEM((SHARE, D), F32),
         pltpu.SMEM(tile_src.shape, I32),
         pltpu.SMEM(tile_count.shape, I32),
         pltpu.VMEM(features.shape, F32),
@@ -413,7 +412,7 @@
         pltpu.VMEM((8, TILE), F32),
         pltpu.VMEM((N_Z, 8, TILE), F32),
         pltpu.VMEM((N_X, 8, TILE), F32),
-        pltpu.SemaphoreType.DMA((12,)),
+        pltpu.SemaphoreType.DMA((15,)),
         pltpu.SemaphoreType.DMA((14,)),
         pltpu.SemaphoreType.DMA((14,)),
     ]

time: 66.4 us -> 66.4 us (level)
  no operation moved by 1% of the time
where the time goes in v6:
time: 66.4 us; the launch traced here: 65.8 us
  Pallas kernels  64.5 us (97%)
  between operations  1.29 us (2%)
    pallas_call x1, Pallas kernels, on_device(): pl.pallas_call(kernel, out_shape=results, in_specs=[hbm] * 9, out_specs=(...  62.9 us
    pallas_call x1, Pallas kernels, on_device(): pl.pallas_call(hand_on, out_shape=results, in_specs=[hbm, hbm], out_specs...  1.6 us

profile of v6, /device:TPU:1, one launch (start us, length us, event | category | flops | bytes accessed | tf_op | source)
XLA Modules:
  0.0 65.8 jit_solution(5928297679047619213)
XLA Ops:
  1.3 62.9 %shard_map.104 = (f32[256,128]{1,0:T(8,128)}, f32[16,256]{1,0:T(8,128)}) custom-call(s32[1,6]{1,0:T(1,128)} %tile_src_hbm.1, s32[1]{0:T(128)S(6)} %copy.11.tile_count_hbm, f32[16,2048]{1,0:T(8,128)} %features_hbm.1, s32[32,48]{1,0:T(8,128)} %bitcast.3, s32[768]{0:T(1024)} %hub_owner_hbm.1, s32[768]{0:T(1024)} %hub_row_hbm.1, f32[16,256]{1,0:T(8,128)} %bitcast.4, ...), custom_call_target="tpu_custom_call" | custom-call | tf_op jit(solution)/shard_map/pallas_call | solution.py:423
  64.2 1.6 %shard_map.105 = (f32[256,128]{1,0:T(8,128)}, f32[16,256]{1,0:T(8,128)}) custom-call(f32[256,128]{1,0:T(8,128)} %get-tuple-element.6.output, f32[16,256]{1,0:T(8,128)} %get-tuple-element.7.grad_weight), custom_call_target="tpu_custom_call" | custom-call | tf_op jit(solution)/shard_map/pallas_call | solution.py:435
